TPU v7x, 256 devices: a whole 4x4x8 slice. The times are simulated.
256 devices in a mesh: gx: 16 (over x, y_lo, core), gy: 16 (over z, y_hi).
Axes of the slice: x: 4, y: 4 (y_hi: 2, y_lo: 2; y = y_hi * 2 + y_lo), z: 8, core: 2. Of those that a mesh axis runs over, the one named last changes fastest.
Arguments:
- tokens: bfloat16 [512, 16384], P('gy', 'gx'), may hold values from -6 to 6
- gate_weight: bfloat16 [16384, 26624], P('gx', 'gy'), may hold values from -0.046875 to 0.046875
- up_weight: bfloat16 [16384, 26624], P('gx', 'gy'), may hold values from -0.046875 to 0.046875
- down_weight: bfloat16 [26624, 16384], P('gy', 'gx'), may hold values from -0.0390625 to 0.0390625
Outputs:
- block_out: bfloat16 [512, 16384], P('gy', 'gx')
All inputs are finite; a program needn't handle non-finite values.
Results may differ from a plain program's by a relative error of at most 0.0039.
Values may be sent and summed in bfloat16 or wider, within the bound.
A program may use at most 64 MiB of HBM per device.

v0:
```python
import jax
import jax.numpy as jnp
from jax import lax
from jax.sharding import PartitionSpec as P


def on_device(tokens, gate_weight, up_weight, down_weight):
    columns = lax.all_gather(tokens, "gy", axis=0, tiled=True)
    width = gate_weight.shape[1]
    gate_term = jnp.dot(columns, gate_weight, preferred_element_type=jnp.float32)
    up_term = jnp.dot(columns, up_weight, preferred_element_type=jnp.float32)
    summed = lax.psum(jnp.concatenate([gate_term, up_term], axis=1), "gx")
    hidden = (jax.nn.silu(summed[:, :width]) * summed[:, width:]).astype(jnp.bfloat16)
    terms = jnp.dot(hidden, down_weight, preferred_element_type=jnp.float32)
    own_rows = lax.psum_scatter(terms, "gy", scatter_dimension=0, tiled=True)
    return (tokens.astype(jnp.float32) + own_rows).astype(jnp.bfloat16)


def solution(mesh):
    in_specs = (P("gy", "gx"), P("gx", "gy"), P("gx", "gy"), P("gy", "gx"))
    out_specs = P("gy", "gx")
    return jax.shard_map(
        on_device, mesh=mesh, in_specs=in_specs, out_specs=out_specs, check_vma=False
    )
```

profile of v0, /device:TPU:4, one launch (start us, length us, event | category | flops | bytes accessed | tf_op | source)
XLA Modules:
  0.0 490.2 jit_solution(3387234217459637286)
XLA Ops:
  6.5 0.0 copy-start
  6.5 0.0 all-gather.2.cloned.1.call-start
  6.5 0.7 all-gather.2.cloned.1.call-update
  7.3 0.0 all-reduce.2.cloned.1.call-start
  7.3 84.4 %all-gather.2.cloned.1.call-done = bf16[512,1024]{1,0:T(8,128)(2,1)} async-done(((bf16[32,1024]{1,0:T(8,128)(2,1)}), bf16[512,1024]{1,0:T(8,128)(2,1)}) %all-gather.2.cloned.1.call-update) | async-done | bytes 1048592 | tf_op jit(solution)/shard_map/all_gather | solution.py:8
  91.7 0.0 copy-done
  91.7 0.0 copy-start.2
  91.7 0.0 copy-start.3
  91.7 3.4 fusion.5
  95.2 0.0 copy-done.2
  95.2 0.0 copy-done.3
  95.2 2.1 fusion.4
  97.3 3.4 pad_maximum_fusion
  100.6 0.0 all-reduce.2.cloned.1.call-update
  100.7 0.0 copy-start.1
  100.7 0.0 reduce-scatter.2.cloned.1.call-start
  100.7 164.3 %all-reduce.2.cloned.1.call-done = f32[512,3328]{1,0:T(8,128)} async-done(((f32[512,3328]{1,0:T(8,128)}), f32[512,3328]{1,0:T(8,128)}) %all-reduce.2.cloned.1.call-update) | async-done | bytes 6815760 | tf_op jit(solution)/shard_map/psum | solution.py:12
  265.0 7.5 %fusion.1 = f32[512,1024]{1,0:T(8,128)} fusion(bf16[1664,1024]{1,0:T(8,128)(2,1)} %param.7, f32[512,3328]{1,0:T(8,128)} %all-reduce.2.cloned.1.call-done), kind=kOutput, calls=%fused_computation.3 | convolution fusion | flops 1749942272 | bytes 12320768 | tf_op jit(solution)/shard_map/dot_general | solution.py:14
  272.5 0.0 reduce-scatter.2.cloned.1.call-update
  272.5 209.6 %reduce-scatter.2.cloned.1.call-done = f32[32,1024]{1,0:T(8,128)} async-done(((f32[512,1024]{1,0:T(8,128)}), f32[32,1024]{1,0:T(8,128)}) %reduce-scatter.2.cloned.1.call-update) | async-done | bytes 131088 | tf_op jit(solution)/shard_map/reduce_scatter | solution.py:15
  482.1 0.0 copy-done.1
  482.1 1.5 add_convert_fusion
Async XLA Ops:
  6.5 85.2 %copy-start = (bf16[1024,1664]{1,0:T(8,128)(2,1)S(1)}, bf16[1024,1664]{1,0:T(8,128)(2,1)}, u32[]{:S(2)}) copy-start(bf16[1024,1664]{1,0:T(8,128)(2,1)} %param.6) | copy-start | bytes 10223620
  6.5 85.2 %all-gather.2.cloned.1.call-start = ((), (), s32[]{:S(2)}) async-start(), calls=%async_computation.1 | async-start | bytes 1114112 | tf_op jit(solution)/shard_map/all_gather | solution.py:8
  7.3 257.7 %all-reduce.2.cloned.1.call-start = ((), (), s32[]{:S(2)}) async-start(), calls=%async_computation.2 | async-start | bytes 13631488 | tf_op jit(solution)/shard_map/psum | solution.py:12
  91.7 3.4 copy-start.2
  91.7 3.5 copy-start.3
  100.7 381.5 %copy-start.1 = (bf16[32,1024]{1,0:T(8,128)(2,1)S(1)}, bf16[32,1024]{1,0:T(8,128)(2,1)}, u32[]{:S(2)}) copy-start(bf16[32,1024]{1,0:T(8,128)(2,1)} %param.4) | copy-start | bytes 196612
  100.7 381.5 %reduce-scatter.2.cloned.1.call-start = ((), (), s32[]{:S(2)}) async-start(), calls=%async_computation.3 | async-start | bytes 2228224 | tf_op jit(solution)/shard_map/reduce_scatter | solution.py:15
Sparse Core Ops, SparseCore 0:
  9.9 81.7 all-gather.1
  100.8 164.1 all-reduce.1
  272.6 209.4 reduce-scatter.1
where the time goes:
time: 490 us
  waiting for transfers between devices  459 us (94%)
  between operations  13.1 us (3%)
  matrix products  13 us (3%)
  other arithmetic  4.9 us (1%)
    reduce_scatter x1, waiting for transfers between devices, on_device(): own_rows = lax.psum_scatter(terms, 'gy', scatter_dimension=0, tiled=True)  210 us
    psum x1, waiting for transfers between devices, on_device(): summed = lax.psum(jnp.concatenate([gate_term, up_term], axis=1), 'gx')  164 us
    all_gather x1, waiting for transfers between devices, on_device(): columns = lax.all_gather(tokens, 'gy', axis=0, tiled=True)  84.4 us
  transfers between devices with their start and end apart: 3, of which 3 were waited for; matrix products, arithmetic and copies ran while one was open for 0% of the time, Pallas kernels for 0%

commit v1 on v0

v1 whole, which is shorter than its diff:
```python
import jax
import jax.numpy as jnp
from jax import lax
from jax.experimental import pallas as pl
from jax.experimental.pallas import tpu as pltpu
from jax.sharding import PartitionSpec as P

MESH = pl.DeviceIdType.MESH
BF16 = jnp.bfloat16
F32 = jnp.float32

ROWS = 32
PIECE = 16
LANES = 128
TILES = 13
FF = TILES * LANES
HALF = 512
GROUPS = ((0, 7), (7, 13))
CUT = 7 * LANES
N_SEMS = 160


def block_kernel(
    tokens, wg, wu, wd, out,
    w_gu, w_dn, tok, acc, xs, xr, sg, su, rg, gys, gyr, g_own, ru, us, u_own, rx, hid,
    o_f, sa1, ra1, sa2, ra2, sa3, ra3, sa4, ra4, ya_s, ya_r, yb_s, yb_r, b_f,
    sb1, rb1, sb2, rb2, sb3, rb3, sb4, rb4, w_sem, d_sem, t_sem, ss, rs,
):
    gx, gy = lax.axis_index("gx"), lax.axis_index("gy")
    x, yl, c = lax.div(gx, 4), lax.rem(lax.div(gx, 2), 2), lax.rem(gx, 2)
    z, yh = lax.div(gy, 2), lax.rem(gy, 2)

    def xat(k):
        return lax.rem(x + k + 4, 4)

    def zat(k):
        return lax.rem(z + k + 8, 8)

    def to_x(k):
        return (xat(k) * 4 + yl * 2 + c, gy)

    def to_z(k):
        return (gx, zat(k) * 2 + yh)

    to_yl = (x * 4 + (1 - yl) * 2 + c, gy)
    to_core = (x * 4 + yl * 2 + (1 - c), gy)
    to_yh = (gx, z * 2 + (1 - yh))

    t_copy = pltpu.make_async_copy(tokens, tok.at[yh], t_sem)
    t_copy.start()

    def w_copy(g, i):
        lo, hi = GROUPS[g]
        n = (hi - lo) * LANES
        return pltpu.make_async_copy(
            (wg, wu)[i].at[:, pl.ds(lo * LANES, n)],
            w_gu.at[:, pl.ds(2 * lo * LANES + i * n, n)],
            w_sem.at[g, i],
        )

    d_copy = pltpu.make_async_copy(wd, w_dn, d_sem)

    barrier = pltpu.get_barrier_semaphore()
    peers = [to_z(1), to_z(-1), to_yh, to_z(2), to_z(-2), to_x(1), to_x(3), to_x(2), to_yl, to_core]
    for p in peers:
        pl.semaphore_signal(barrier, inc=1, device_id=p, device_id_type=MESH)
    t_copy.wait()
    pl.semaphore_wait(barrier, len(peers))

    sent = []
    count = [0]

    def send(src, dst, device):
        i = count[0]
        count[0] += 1
        cp = pltpu.make_async_remote_copy(
            src_ref=src, dst_ref=dst, send_sem=ss.at[i], recv_sem=rs.at[i],
            device_id=device, device_id_type=MESH,
        )
        cp.start()
        sent.append(cp)
        return cp


    def pass_on(slot):
        return send(tok.at[slot], tok.at[slot], to_yh)

    def near_two(a):
        return send(tok.at[a], tok.at[6 + a], to_z(4 * a - 2))

    def far_two(a):
        return send(tok.at[a], tok.at[8 + a], to_z(2 - 4 * a))

    def forward_near(a):
        rows = pl.ds(pl.multiple_of((1 - a) * PIECE, PIECE), PIECE)
        return [
            send(tok.at[6 + a], tok.at[10 + 3 * a], to_z(2 * a - 1)),
            send(tok.at[6 + a, rows], tok.at[14 + a, rows], to_z(4 * a - 2)),
        ]

    def forward_far(a):
        rows = pl.ds(pl.multiple_of(a * PIECE, PIECE), PIECE)
        return [
            send(tok.at[8 + a], tok.at[12 - a], to_z(1 - 2 * a)),
            send(tok.at[8 + a, rows], tok.at[14 + a, rows], to_z(2 - 4 * a)),
        ]

    yo = 1 - yh
    y_0 = pass_on(yh)
    z_r = send(tok.at[yh], tok.at[4 + yh], to_z(1))
    z_l = send(tok.at[yh], tok.at[2 + yh], to_z(-1))
    z_n = near_two(yh)
    for g in range(2):
        for i in range(2):
            w_copy(g, i).start()
    z_f = far_two(yh)
    y_0.wait_recv()
    z_no = near_two(yo)
    z_fo = far_two(yo)
    z_r.wait_recv()
    y_r = pass_on(4 + yh)
    z_l.wait_recv()
    y_l = pass_on(2 + yh)
    z_n.wait_recv()
    z_34 = forward_near(yh)
    z_f.wait_recv()
    z_34 += forward_far(yh)
    y_n = [y_r, y_l, z_no]

    def far_tokens():
        z = forward_near(yo)
        z_fo.wait_recv()
        return z_34 + z + forward_far(yo)

    def products(k, waits):
        cps = []
        for cp in waits:
            cp.wait_recv()
        rows = tok[pl.ds(8 * k, 8)].reshape(256, 1024)
        for g, (lo, hi) in enumerate(GROUPS):
            if k == 0:
                for i in range(2):
                    w_copy(g, i).wait()
            n = (hi - lo) * 256
            acc[g, :, :, pl.ds(0, n)] = jnp.dot(
                rows, w_gu[:, lo * 256 : hi * 256], preferred_element_type=F32
            ).reshape(2, 128, n)
            xs[k, g, :, pl.ds(0, n)] = acc[g, 1 - c, :, pl.ds(0, n)].astype(BF16)
            cps.append(
                send(xs.at[k, g, :, pl.ds(0, n)], xr.at[k, g, :, pl.ds(0, n)], to_core)
            )
        return cps

    def pair_sums(k, cps):
        gate_x, up_y = [], []
        for g, (lo, hi) in enumerate(GROUPS):
            cps[g].wait_recv()

            def add(t, carry):
                def total(i):
                    start = (t - lo + i * (hi - lo)) * LANES
                    cols = pl.ds(pl.multiple_of(start, LANES), LANES)
                    v = acc[g, c, :, cols] + xr[k, g, :, cols].astype(F32)
                    return v.reshape(4, 2, PIECE, LANES).astype(BF16)

                sg[k, t] = total(0)
                su[k, t] = total(1)
                return carry

            lax.fori_loop(lo, hi, add, 0)
            ts = pl.ds(lo, hi - lo)
            up_y.append(send(su.at[k, ts, :, 1 - yl], ru.at[k, ts], to_yl))
            gate_x.append(
                [send(sg.at[k, ts, xat(j)], rg.at[k, j - 1, ts], to_x(j)) for j in (1, 3, 2)]
            )
        return gate_x, up_y

    def chip_sums(k, gate_x, up_y):
        gate_y, up_x = [], []
        for g, (lo, hi) in enumerate(GROUPS):
            ts = pl.ds(lo, hi - lo)
            up_y[g].wait_recv()

            def add_up(t, carry):
                us[k, t] = (su[k, t, :, yl].astype(F32) + ru[k, t].astype(F32)).astype(BF16)
                u_own[k, t] = su[k, t, x, yl].astype(F32) + ru[k, t, x].astype(F32)
                return carry

            lax.fori_loop(lo, hi, add_up, 0)
            up_x.append(
                [send(us.at[k, ts, xat(j)], rx.at[k, j - 1, ts], to_x(j)) for j in (1, 3, 2)]
            )
            for cp in gate_x[g]:
                cp.wait_recv()

            def add_gate(t, carry):
                def total(y):
                    return (
                        sg[k, t, x, y].astype(F32) + rg[k, 0, t, y].astype(F32)
                        + rg[k, 1, t, y].astype(F32) + rg[k, 2, t, y].astype(F32)
                    )

                gys[k, t] = total(1 - yl).astype(BF16)
                g_own[k, t] = total(yl)
                return carry

            lax.fori_loop(lo, hi, add_gate, 0)
            gate_y.append(send(gys.at[k, ts], gyr.at[k, ts], to_yl))
        return gate_y, up_x

    h0, h1 = pl.ds(0, CUT), pl.ds(CUT, FF - CUT)
    every = slice(None)

    def activate(k, g, gate_y, up_x):
        lo, hi = GROUPS[g]
        gate_y[g].wait_recv()
        for cp in up_x[g]:
            cp.wait_recv()
        for t in range(lo, hi):
            gate = g_own[k, t] + gyr[k, t].astype(F32)
            up = (
                u_own[k, t] + rx[k, 0, t].astype(F32) + rx[k, 1, t].astype(F32)
                + rx[k, 2, t].astype(F32)
            )
            h = gate / (1.0 + jnp.exp(-gate)) * up
            hid[k, c, x, yl, :, pl.ds(t * LANES, LANES)] = h.astype(BF16)

    def share(index, device):
        return send(hid.at[index], hid.at[index], device)

    def spread(k, gate_y, up_x):
        activate(k, 0, gate_y, up_x)
        mine = (k, c, x, yl, every, h0)
        p_y = [share(mine, to_yl)]
        p_x = [share(mine, to_x(j)) for j in (1, 3, 2)]
        p_c = [share(mine, to_core)]
        activate(k, 1, gate_y, up_x)
        q_y = share((k, c, x, yl, every, h1), to_yl)
        return p_x, p_y, p_c, q_y

    def spread_on(k, p_x, p_y, p_c, q_y):
        q_y.wait_recv()
        both = (k, c, x, every, every, h1)
        q_x = [share(both, to_x(j)) for j in (1, 3, 2)]
        p_c.append(share(both, to_core))
        for i, j in enumerate((1, 3, 2)):
            p_x[i].wait_recv()
            piece = (k, c, xat(-j), yl, every, h0)
            p_y.append(share(piece, to_yl))
            p_c.append(share(piece, to_core))
        return p_y, q_x, p_c

    def spread_last(k, p_y, q_x, p_c):
        for i, j in enumerate((0, 1, 3, 2)):
            p_y[i].wait_recv()
            p_c.append(share((k, c, xat(-j), 1 - yl, every, h0), to_core))
        for i, j in enumerate((1, 3, 2)):
            q_x[i].wait_recv()
            p_c.append(share((k, c, xat(-j), every, every, h1), to_core))
        return p_c

    ca, cb = pl.ds(0, HALF), pl.ds(HALF, HALF)

    def down(k, cols):
        o_f[pl.ds(4 * k, 4), :, :, cols] = jnp.dot(
            hid[k].reshape(256, FF), w_dn[:, cols], preferred_element_type=F32
        ).reshape(4, 2, ROWS, HALF)

    def part(slot, cols):
        return o_f[slot // 2, slot % 2, :, cols]

    def put(buf, value, device, dst):
        buf[...] = value.astype(BF16)
        return send(buf, dst, device)

    def y_first(k):
        return put(yb_s.at[k], o_f[pl.ds(4 * k, 4), 1 - yh, :, cb], to_yh, yb_r.at[k])

    def y_add(k, cp):
        cp.wait_recv()
        ks = pl.ds(4 * k, 4)
        b_f[ks] = o_f[ks, yh, :, cb] + yb_r[k].astype(F32)

    for cp in y_n:
        cp.wait_recv()
    y_f = far_tokens()
    core_0 = products(0, [])
    d_copy.start()
    gate_x0, up_y0 = pair_sums(0, core_0)
    core_1 = products(1, y_f)
    gate_y0, up_x0 = chip_sums(0, gate_x0, up_y0)
    gate_x1, up_y1 = pair_sums(1, core_1)
    spread_0 = spread(0, gate_y0, up_x0)
    gate_y1, up_x1 = chip_sums(1, gate_x1, up_y1)
    on_0 = spread_on(0, *spread_0)
    spread_1 = spread(1, gate_y1, up_x1)
    p_c0 = spread_last(0, *on_0)
    d_copy.wait()
    on_1 = spread_on(1, *spread_1)
    for cp in p_c0:
        cp.wait_recv()
    down(0, ca)
    a_1r = put(sa1.at[0], o_f[1, :, :, ca], to_z(1), ra1.at[0])
    a_1l = put(sa1.at[1], o_f[2, :, :, ca], to_z(-1), ra1.at[1])
    p_c1 = spread_last(1, *on_1)
    down(0, cb)
    b_y0 = y_first(0)
    for cp in p_c1:
        cp.wait_recv()
    down(1, cb)
    b_y1 = y_first(1)
    down(1, ca)
    a_3r = put(sa3.at[0], o_f[5, :, :, ca], to_z(1), ra3.at[0])
    a_3l = put(sa3.at[1], o_f[6, :, :, ca], to_z(-1), ra3.at[1])
    a_4r = put(sa4.at[0], part(14, ca), to_z(2), ra4.at[0])
    a_4l = put(sa4.at[1], part(15, ca), to_z(-2), ra4.at[1])
    y_add(0, b_y0)
    b_1r = put(sb1.at[0], b_f[1], to_z(1), rb1.at[0])
    b_1l = put(sb1.at[1], b_f[2], to_z(-1), rb1.at[1])
    y_add(1, b_y1)
    top, low = pl.ds(0, PIECE), pl.ds(PIECE, PIECE)
    b_3r = put(sb3.at[0], b_f[5], to_z(1), rb3.at[0])
    b_3l = put(sb3.at[1], b_f[6], to_z(-1), rb3.at[1])
    b_4r = put(sb4.at[0], b_f[7, top], to_z(2), rb4.at[0])
    b_4l = put(sb4.at[1], b_f[7, low], to_z(-2), rb4.at[1])
    a_3r.wait_recv()
    a_4r.wait_recv()
    sa2[0, 0] = (part(6, ca) + ra3[0, 0].astype(F32) + ra4[0].astype(F32)).astype(BF16)
    sa2[0, 1] = (part(9, ca) + ra3[0, 1].astype(F32)).astype(BF16)
    a_2r = send(sa2.at[0], ra2.at[0], to_z(2))
    a_3l.wait_recv()
    a_4l.wait_recv()
    sa2[1, 0] = (part(8, ca) + ra3[1, 0].astype(F32)).astype(BF16)
    sa2[1, 1] = (part(7, ca) + ra3[1, 1].astype(F32) + ra4[1].astype(F32)).astype(BF16)
    a_2l = send(sa2.at[1], ra2.at[1], to_z(-2))
    b_3r.wait_recv()
    b_4r.wait_recv()
    two_r, two_l = 3 + yh, 4 - yh
    sb2[0, top] = (
        b_f[two_r, top] + rb3[0, top].astype(F32) + rb4[0].astype(F32)
    ).astype(BF16)
    sb2[0, low] = (b_f[two_r, low] + rb3[0, low].astype(F32)).astype(BF16)
    b_2r = send(sb2.at[0], rb2.at[0], to_z(2))
    b_3l.wait_recv()
    b_4l.wait_recv()
    sb2[1, top] = (b_f[two_l, top] + rb3[1, top].astype(F32)).astype(BF16)
    sb2[1, low] = (
        b_f[two_l, low] + rb3[1, low].astype(F32) + rb4[1].astype(F32)
    ).astype(BF16)
    b_2l = send(sb2.at[1], rb2.at[1], to_z(-2))
    for cp in (a_1r, a_1l, a_2r, a_2l):
        cp.wait_recv()

    def a_total(y):
        total = o_f[0, y, :, ca]
        for r in (ra1, ra2):
            total = total + r[0, y].astype(F32) + r[1, y].astype(F32)
        return total

    a_y = put(ya_s, a_total(1 - yh), to_yh, ya_r)
    mine_a = tok[yh, :, ca].astype(F32) + a_total(yh)
    for cp in (b_1r, b_1l, b_2r, b_2l):
        cp.wait_recv()
    mine_b = b_f[0]
    for r in (rb1, rb2):
        mine_b = mine_b + r[0].astype(F32) + r[1].astype(F32)
    out[:, cb] = (tok[yh, :, cb].astype(F32) + mine_b).astype(BF16)
    a_y.wait_recv()
    out[:, ca] = (mine_a + ya_r[...].astype(F32)).astype(BF16)

    for cp in sent:
        cp.wait_send()


def on_device(tokens, gate_weight, up_weight, down_weight):
    vmem = pl.BlockSpec(memory_space=pltpu.VMEM)
    hbm = pl.BlockSpec(memory_space=pltpu.HBM)
    tile = (PIECE, LANES)

    def buf(*shape, dtype=BF16):
        return pltpu.VMEM(shape, dtype)

    return pl.pallas_call(
        block_kernel,
        out_shape=jax.ShapeDtypeStruct(tokens.shape, BF16),
        in_specs=[hbm] * 4,
        out_specs=vmem,
        scratch_shapes=[
            buf(1024, 2 * FF),
            buf(FF, 1024),
            buf(16, ROWS, 1024),
            buf(2, 2, 128, 1792, dtype=F32),
            buf(2, 2, 128, 1792),
            buf(2, 2, 128, 1792),
            buf(2, TILES, 4, 2, *tile),
            buf(2, TILES, 4, 2, *tile),
            buf(2, 3, TILES, 2, *tile),
            buf(2, TILES, *tile),
            buf(2, TILES, *tile),
            buf(2, TILES, *tile, dtype=F32),
            buf(2, TILES, 4, *tile),
            buf(2, TILES, 4, *tile),
            buf(2, TILES, *tile, dtype=F32),
            buf(2, 3, TILES, *tile),
            buf(2, 2, 4, 2, PIECE, FF),
            buf(8, 2, ROWS, 1024, dtype=F32),
            buf(2, 2, ROWS, HALF),
            buf(2, 2, ROWS, HALF),
            buf(2, 2, ROWS, HALF),
            buf(2, 2, ROWS, HALF),
            buf(2, 2, ROWS, HALF),
            buf(2, 2, ROWS, HALF),
            buf(2, ROWS, HALF),
            buf(2, ROWS, HALF),
            buf(ROWS, HALF),
            buf(ROWS, HALF),
            buf(2, 4, ROWS, HALF),
            buf(2, 4, ROWS, HALF),
            buf(8, ROWS, HALF, dtype=F32),
            buf(2, ROWS, HALF),
            buf(2, ROWS, HALF),
            buf(2, ROWS, HALF),
            buf(2, ROWS, HALF),
            buf(2, ROWS, HALF),
            buf(2, ROWS, HALF),
            buf(2, PIECE, HALF),
            buf(2, PIECE, HALF),
            pltpu.SemaphoreType.DMA((2, 2)),
            pltpu.SemaphoreType.DMA,
            pltpu.SemaphoreType.DMA,
            pltpu.SemaphoreType.DMA((N_SEMS,)),
            pltpu.SemaphoreType.DMA((N_SEMS,)),
        ],
        compiler_params=pltpu.CompilerParams(
            collective_id=0, has_side_effects=True, vmem_limit_bytes=52 * 2**20
        ),
        cost_estimate=pl.CostEstimate(
            flops=5_300_000_000, bytes_accessed=10_500_000, transcendentals=60_000
        ),
    )(tokens, gate_weight, up_weight, down_weight)


def solution(mesh):
    in_specs = (P("gy", "gx"), P("gx", "gy"), P("gx", "gy"), P("gy", "gx"))
    return jax.shard_map(
        on_device, mesh=mesh, in_specs=in_specs, out_specs=P("gy", "gx"), check_vma=False
    )
```

time: 490 us -> 72.4 us (0.15)
  waiting for transfers between devices: 459 us -> 0 us
  Pallas kernels: 0 us -> 69.7 us
  between operations: 13.1 us -> 0.01 us
  matrix products: 13 us -> 0 us
  other arithmetic: 4.9 us -> 0 us
    reduce_scatter x1 -> x0, waiting for transfers between devices: 210 us -> none  [on_device(): own_rows = lax.psum_scatter(terms, 'gy', scatter_dimension=0, tiled=True)]
    psum x1 -> x0, waiting for transfers between devices: 164 us -> none  [on_device(): summed = lax.psum(jnp.concatenate([gate_term, up_term], axis=1), 'gx')]
    all_gather x1 -> x0, waiting for transfers between devices: 84.4 us -> none  [on_device(): columns = lax.all_gather(tokens, 'gy', axis=0, tiled=True)]
    pallas_call x0 -> x1, Pallas kernels: none -> 69.7 us  [on_device(): pl.pallas_call(block_kernel, out_shape=jax.ShapeDtypeStruct(tokens.shape,...]
    dot_general x3 -> x0, matrix products: 13 us -> none  [the longest x1 7.48 us: on_device(): terms = jnp.dot(hidden, down_weight, preferred_element_type=jnp.float32)]
  transfers between devices with their start and end apart: 3 -> 0, of which waited for: 3 -> 0; matrix products, arithmetic and copies ran while one was open for 0% -> 0% of each run, Pallas kernels for 0% -> 0%
where the time goes in v1:
time: 72.4 us; the launch traced here: 71.1 us
  Pallas kernels  69.7 us (96%)
  local copies, waits for them, and re-layouts  1.47 us (2%)
    pallas_call x1, Pallas kernels, on_device(): pl.pallas_call(block_kernel, out_shape=jax.ShapeDtypeStruct(tokens.shape,...  69.7 us
    unnamed x3, local copies, waits for them, and re-layouts  1.47 us

profile of v1, /device:TPU:4, one launch (start us, length us, event | category | flops | bytes accessed | tf_op | source)
XLA Modules:
  0.0 71.1 jit_solution(12769900459077974444)
XLA Ops:
  0.0 0.0 copy-start
  0.0 0.8 %copy-done = bf16[32,1024]{1,0:T(8,128)(2,1)S(1)} copy-done((bf16[32,1024]{1,0:T(8,128)(2,1)S(1)}, bf16[32,1024]{1,0:T(8,128)(2,1)}, u32[]{:S(2)}) %copy-start) | copy-done | bytes 65560
  0.8 69.7 %shard_map.46 = bf16[32,1024]{1,0:T(8,128)(2,1)S(1)} custom-call(bf16[32,1024]{1,0:T(8,128)(2,1)S(1)} %copy-done, bf16[1024,1664]{1,0:T(8,128)(2,1)} %wg.1, bf16[1024,1664]{1,0:T(8,128)(2,1)} %wu.1, bf16[1664,1024]{1,0:T(8,128)(2,1)} %wd.1), custom_call_target="tpu_custom_call" | custom-call | flops 5299999744 | bytes 10500000 | tf_op jit(solution)/shard_map/pallas_call | solution.py:383
  70.5 0.6 copy.6
Async XLA Ops:
  0.0 0.8 %copy-start = (bf16[32,1024]{1,0:T(8,128)(2,1)S(1)}, bf16[32,1024]{1,0:T(8,128)(2,1)}, u32[]{:S(2)}) copy-start(bf16[32,1024]{1,0:T(8,128)(2,1)} %tokens.1) | copy-start | bytes 196612
